TPU v7x, 32 devices: a whole 2x2x4 slice. The times are simulated.
32 devices in a mesh: tensor: 4 (over y, core), adapter: 8 (over z, x).
Axes of the slice: x: 2, y: 2, z: 4, core: 2. Of those that a mesh axis runs over, the one named last changes fastest.
Arguments:
- tokens_in: bfloat16 [128, 8192], P(('tensor', 'adapter')), may hold values from -6 to 6
- w_gate: bfloat16 [8192, 28672], P(None, ('tensor', 'adapter')), may hold values from -0.0625 to 0.0625
- w_up: bfloat16 [8192, 28672], P(None, ('tensor', 'adapter')), may hold values from -0.0625 to 0.0625
- w_down: bfloat16 [28672, 8192], P('tensor', 'adapter'), may hold values from -0.03125 to 0.03125
- a_gate: bfloat16 [8192, 1024], P(None, 'adapter'), may hold values from -0.0625 to 0.0625
- a_up: bfloat16 [8192, 1024], P(None, 'adapter'), may hold values from -0.0625 to 0.0625
- b_gate: bfloat16 [1024, 28672], P(None, ('tensor', 'adapter')), may hold values from -1.5 to 1.5
- b_up: bfloat16 [1024, 28672], P(None, ('tensor', 'adapter')), may hold values from -1.5 to 1.5
- a_down: bfloat16 [28672, 1024], P(('tensor', 'adapter')), may hold values from -0.03125 to 0.03125
- b_down: bfloat16 [1024, 8192], P('adapter'), may hold values from -1.5 to 1.5
- lengths: int32 [8], replicated, may hold values from 1 to 32, 128 in all
- request_adapter: int32 [8], replicated, may hold values from 0 to 63
- placement: int32 [64], replicated, may hold values from 0 to 63, each once
Outputs:
- mixed: bfloat16 [128, 8192], P(('tensor', 'adapter'))
Inputs may be any that keep to these rules, and one draw needn't show every extreme that they name: The 8 lengths sum to 128; the longest is exactly 128 // 4. `placement`: each storage slot holds exactly one adapter.
All inputs are finite; a program needn't handle non-finite values.
Results may differ from a plain program's by a relative error of at most 0.0085.
Values may be sent and summed in bfloat16 or wider, within the bound.
A program may use at most 128 MiB of HBM per device.

v0:
```python
import jax
import jax.numpy as jnp
from jax import lax
from jax.sharding import PartitionSpec as P

R = 16
ADP_DEV = 8


def token_tables(lengths, request_adapter, placement, all_tokens):
    positions = jnp.arange(all_tokens, dtype=jnp.int32)
    request_ends = jnp.cumsum(lengths)
    request = jnp.sum((positions[:, None] >= request_ends[None, :]).astype(jnp.int32), axis=1)
    request_hot = request[:, None] == jnp.arange(lengths.shape[0], dtype=jnp.int32)[None, :]
    adapter = jnp.sum(jnp.where(request_hot, request_adapter[None, :], 0), axis=1)
    adapter_hot = adapter[:, None] == jnp.arange(placement.shape[0], dtype=jnp.int32)[None, :]
    slot_index = jnp.sum(jnp.where(adapter_hot, placement[None, :], 0), axis=1)
    return (adapter_hot, slot_index)


def spread_block(low_rank, hot_rows):
    spread = jnp.where(
        hot_rows[:, :, None], low_rank[:, None, :], jnp.zeros_like(low_rank)[:, None, :]
    )
    return spread.reshape(low_rank.shape[0], -1)


def owner_shrink(rows_in, a_gate, a_up):
    return jnp.concatenate(
        [
            jnp.dot(rows_in, a_gate, preferred_element_type=jnp.float32),
            jnp.dot(rows_in, a_up, preferred_element_type=jnp.float32),
        ],
        axis=1,
    )


def local(
    tokens_in,
    w_gate,
    w_up,
    w_down,
    a_gate,
    a_up,
    b_gate,
    b_up,
    a_down,
    b_down,
    lengths,
    request_adapter,
    placement,
):
    n_tensor = lax.axis_size("tensor")
    n_adapter = lax.axis_size("adapter")
    tok_dev = tokens_in.shape[0]
    all_tokens = tok_dev * n_tensor * n_adapter
    group_rows = tok_dev * n_adapter
    adapter_count = placement.shape[0]
    adapter_hot, slot_index = token_tables(lengths, request_adapter, placement, all_tokens)
    group_start = lax.axis_index("tensor") * group_rows
    group_slot = lax.dynamic_slice_in_dim(slot_index, group_start, group_rows)
    owned = group_slot // ADP_DEV == lax.axis_index("adapter")
    local_mask = (group_slot % ADP_DEV)[:, None] == jnp.arange(ADP_DEV, dtype=jnp.int32)[None, :]
    keep_mask = owned[:, None] & local_mask
    rows_group = lax.all_gather(tokens_in, "adapter", axis=0, tiled=True)
    projected = owner_shrink(rows_group, a_gate, a_up).reshape(group_rows, 2, ADP_DEV, R)
    picked = jnp.sum(jnp.where(keep_mask[:, None, :, None], projected, 0.0), axis=2).reshape(
        group_rows, 2 * R
    )
    shrunk_group = lax.psum(picked, "adapter").astype(jnp.bfloat16)
    gathered, shrunk_all = (
        lax.all_gather(rows_group, "tensor", axis=0, tiled=True),
        lax.all_gather(shrunk_group, "tensor", axis=0, tiled=True),
    )
    gate_sum = jnp.dot(gathered, w_gate, preferred_element_type=jnp.float32) + jnp.dot(
        spread_block(shrunk_all[:, :R], adapter_hot), b_gate, preferred_element_type=jnp.float32
    )
    up_sum = jnp.dot(gathered, w_up, preferred_element_type=jnp.float32) + jnp.dot(
        spread_block(shrunk_all[:, R:], adapter_hot), b_up, preferred_element_type=jnp.float32
    )
    hidden = (jax.nn.silu(gate_sum) * up_sum).astype(jnp.bfloat16)
    down_all = jnp.dot(hidden, a_down, preferred_element_type=jnp.float32).reshape(
        all_tokens, adapter_count, R
    )
    low_part = jnp.sum(jnp.where(adapter_hot[:, :, None], down_all, 0.0), axis=1)
    down_full = lax.all_to_all(w_down, "adapter", split_axis=0, concat_axis=1, tiled=True)
    base_part = jnp.dot(hidden, down_full, preferred_element_type=jnp.float32)
    base_sum, low_sum = (
        lax.psum_scatter(base_part, ("tensor", "adapter"), scatter_dimension=0, tiled=True),
        lax.psum_scatter(low_part, ("tensor", "adapter"), scatter_dimension=0, tiled=True),
    )
    low_rank = low_sum.astype(jnp.bfloat16)
    low_group = lax.all_gather(low_rank, "adapter", axis=0, tiled=True)
    spread_low = jnp.where(
        keep_mask[:, :, None], low_group[:, None, :], jnp.zeros_like(low_group)[:, None, :]
    )
    spread_low = spread_low.reshape(group_rows, ADP_DEV * R)
    expanded = jnp.dot(spread_low, b_down, preferred_element_type=jnp.float32).astype(jnp.bfloat16)
    delta_down = lax.psum_scatter(
        expanded.astype(jnp.float32).astype(jnp.bfloat16),
        "adapter",
        scatter_dimension=0,
        tiled=True,
    ).astype(jnp.float32)
    return (base_sum + delta_down).astype(jnp.bfloat16)


def solution(mesh):
    in_specs = (
        P(("tensor", "adapter"), None),
        P(None, ("tensor", "adapter")),
        P(None, ("tensor", "adapter")),
        P("tensor", "adapter"),
        P(None, "adapter"),
        P(None, "adapter"),
        P(None, ("tensor", "adapter")),
        P(None, ("tensor", "adapter")),
        P(("tensor", "adapter"), None),
        P("adapter", None),
        P(),
        P(),
        P(),
    )
    out_specs = P(("tensor", "adapter"), None)
    return jax.shard_map(local, mesh=mesh, in_specs=in_specs, out_specs=out_specs, check_vma=False)
```

profile of v0, /device:TPU:0, one launch (start us, length us, event | category | flops | bytes accessed | tf_op | source)
XLA Modules:
  0.0 703.4 jit_solution(17979303592407708939)
XLA Ops:
  6.5 7.4 %all-to-all-start = ((bf16[8,896,1024]{2,1,0:T(8,128)(2,1)}), bf16[8,896,1024]{2,1,0:T(8,128)(2,1)}, u32[]{:S(2)}, u32[]{:S(2)}) async-start(bf16[8,896,1024]{2,1,0:T(8,128)(2,1)} %bitcast.35), calls=%async_computation | async-start | bytes 29360128 | tf_op jit(solution)/shard_map/all_to_all | solution.py:86
  14.0 339.0 %all-gather = bf16[8,4,8192]{2,1,0:T(4,128)(2,1)S(1)} all-gather(bf16[1,4,8192]{2,1,0:T(4,128)(2,1)S(1)} %bitcast.41), channel_id=1, replica_groups=mesh['tensor'=4,'adapter'=8] {'adapter'}, dimensions={0}, use_global_device_ids=true | all-gather | bytes 589824 | tf_op jit(solution)/shard_map/all_gather | solution.py:65
  353.0 0.9 reshape.155
  354.0 0.2 reduce-window.8
  354.2 2.3 fusion.9
  356.6 0.4 fusion.8
  357.1 0.1 copy.29
  357.3 0.1 select_reduce_fusion.2
  357.4 0.1 fusion.5
  357.6 35.4 %psum.7 = bf16[32,32]{0,1:T(8,128)(2,1)S(1)} all-reduce(f32[32,32]{0,1:T(8,128)S(1)} %bitcast.42), channel_id=1, replica_groups=mesh['tensor'=4,'adapter'=8] {'adapter'}, use_global_device_ids=true, to_apply=%region_5.6 | all-reduce | flops 1024 | bytes 6144 | tf_op jit(solution)/shard_map/psum | solution.py:70
  393.0 0.1 copy.30
  393.1 5.2 all_gather.14
  398.6 8.3 %fusion.7 = f32[128,896]{1,0:T(8,128)S(1)} fusion(bf16[128,8192]{1,0:T(8,128)(2,1)} %all-gather.4.cloned.1.call-done, bf16[8192,896]{1,0:T(8,128)(2,1)} %param.14), kind=kOutput, calls=%fused_computation.30 | convolution fusion | flops 1879048192 | bytes 17235968 | tf_op jit(solution)/shard_map/dot_general | solution.py:75
  406.9 0.5 convolution_add_fusion.1
  407.4 1.1 copy-done.1
  408.5 7.7 %fusion.10 = f32[128,896]{1,0:T(8,128)S(1)} fusion(bf16[128,8192]{1,0:T(8,128)(2,1)S(1)} %copy-done.1, bf16[8192,896]{1,0:T(8,128)(2,1)} %param.15), kind=kOutput, calls=%fused_computation.33 | convolution fusion | flops 1879048192 | bytes 17235968 | tf_op jit(solution)/shard_map/dot_general | solution.py:78
  416.3 0.5 fusion.1
  416.8 1.0 copy-done.4
  417.8 0.8 fusion.12
  418.6 0.1 select_reduce_fusion
  418.7 0.1 copy.35
  418.8 37.2 %all-reduce.1 = bf16[128,16]{1,0:T(8,128)(2,1)S(1)} all-reduce(f32[128,16]{1,0:T(8,128)S(1)} %copy.35), channel_id=3, replica_groups=mesh['tensor'=4,'adapter'=8] {'tensor','adapter'}, use_global_device_ids=true, to_apply=%region_8.9.clone | all-reduce | flops 2048 | bytes 12288
  456.1 20.2 %all-gather.1 = bf16[8,4,16]{2,1,0:T(4,128)(2,1)S(1)} all-gather(bf16[1,4,16]{2,1,0:T(4,128)(2,1)S(1)} %fusion.4), channel_id=1, replica_groups=mesh['tensor'=4,'adapter'=8] {'adapter'}, dimensions={0}, use_global_device_ids=true | all-gather | bytes 1152 | tf_op jit(solution)/shard_map/all_gather | solution.py:93
  476.3 1.3 convolution_convert_fusion
  477.7 0.2 all-reduce.6.cloned.1.call-start
  477.9 19.9 %copy.33 = bf16[896,8,1024]{0,2,1:T(8,128)(2,1)} copy(bf16[896,8,1024]{2,0,1:T(8,128)(2,1)} %bitcast.8) | data formatting | bytes 29360128 | tf_op jit(solution)/shard_map/all_to_all | solution.py:86
  497.8 11.9 %fusion.11 = f32[128,8192]{1,0:T(8,128)} fusion(bf16[128,896]{1,0:T(8,128)(2,1)S(1)} %fusion.1, bf16[896,8192]{0,1:T(8,128)(2,1)} %bitcast.34), kind=kOutput, calls=%fused_computation.34 | convolution fusion | flops 1879048192 | bytes 19103744 | tf_op jit(solution)/shard_map/dot_general | solution.py:87
  509.7 0.6 copy-done.11
  510.4 0.6 dynamic-slice.2
  511.6 35.9 %all-reduce.8.cloned.1.call-done = bf16[32,8192]{1,0:T(8,128)(2,1)} async-done(((bf16[32,8192]{1,0:T(8,128)(2,1)}), bf16[32,8192]{1,0:T(8,128)(2,1)}) %all-reduce.8.cloned.1.call-update) | async-done | bytes 524304
  547.5 147.6 %all-reduce.6.cloned.1.call-done = f32[128,8192]{1,0:T(8,128)} async-done(((f32[128,8192]{1,0:T(8,128)}), f32[128,8192]{1,0:T(8,128)}) %all-reduce.6.cloned.1.call-update) | async-done | bytes 4194320
  695.2 1.7 fusion.2
  (42 shorter events, 0.9 us)
Async XLA Ops:
  6.5 469.8 %copy-start = (bf16[128,8192]{1,0:T(8,128)(2,1)S(1)}, bf16[128,8192]{1,0:T(8,128)(2,1)}, u32[]{:S(2)}) copy-start(bf16[128,8192]{1,0:T(8,128)(2,1)} %param.22) | copy-start | bytes 6291460
  6.5 7.4 %copy-start.6 = (bf16[4,8192]{1,0:T(4,128)(2,1)S(1)}, bf16[4,8192]{1,0:T(4,128)(2,1)}, u32[]{:S(2)}) copy-start(bf16[4,8192]{1,0:T(4,128)(2,1)} %param.13) | copy-start | bytes 196612
  6.5 471.4 %all-to-all-start = ((bf16[8,896,1024]{2,1,0:T(8,128)(2,1)}), bf16[8,896,1024]{2,1,0:T(8,128)(2,1)}, u32[]{:S(2)}, u32[]{:S(2)}) async-start(bf16[8,896,1024]{2,1,0:T(8,128)(2,1)} %bitcast.35), calls=%async_computation | async-start | bytes 29360128 | tf_op jit(solution)/shard_map/all_to_all | solution.py:86
  13.9 340.1 %copy-start.8 = (s32[8]{0:T(128)S(1)}, s32[8]{0:T(128)}, u32[]{:S(2)}) copy-start(s32[8]{0:T(128)} %param.23) | copy-start | bytes 100
  13.9 384.7 %all-gather.4.cloned.1.call-start = ((), (), s32[]{:S(2)}) async-start(), calls=%async_computation.1 | async-start | bytes 2621440 | tf_op jit(solution)/shard_map/all_gather | solution.py:72
  353.9 2.6 copy-start.2
  353.9 193.6 %all-reduce.8.cloned.1.call-start = ((), (), s32[]{:S(2)}) async-start(), calls=%async_computation.3 | async-start | bytes 1048576
  354.2 2.4 copy-start.3
  354.2 3.1 copy-start.9
  354.2 3.1 copy-start.10
  398.6 8.3 %copy-start.5 = (bf16[1024,896]{1,0:T(8,128)(2,1)S(1)}, bf16[1024,896]{1,0:T(8,128)(2,1)}, u32[]{:S(2)}) copy-start(bf16[1024,896]{1,0:T(8,128)(2,1)} %param.19) | copy-start | bytes 5505028
  406.9 1.6 copy-start.1
  408.5 7.8 %copy-start.7 = (bf16[1024,896]{1,0:T(8,128)(2,1)S(1)}, bf16[1024,896]{1,0:T(8,128)(2,1)}, u32[]{:S(2)}) copy-start(bf16[1024,896]{1,0:T(8,128)(2,1)} %param.20) | copy-start | bytes 5505028
  416.3 1.5 copy-start.4
  477.7 217.5 %all-reduce.6.cloned.1.call-start = ((), (), s32[]{:S(2)}) async-start(), calls=%async_computation.2 | async-start | bytes 8388608
  509.7 0.7 copy-start.11
Sparse Core Ops, SparseCore 0:
  354.0 21.8 all-gather.3
  477.8 69.6 all-reduce.7
  554.0 141.1 all-reduce.5
where the time goes:
time: 704 us; the launch traced here: 703 us
  blocking collectives  437 us (62%)
  waiting for transfers between devices  184 us (26%)
  matrix products  33.8 us (5%)
  local copies, waits for them, and re-layouts  24.8 us (4%)
  between operations  14 us (2%)
  starting transfers between devices  7.69 us (1%)
    all_gather x1, blocking collectives, local(): rows_group = lax.all_gather(tokens_in, 'adapter', axis=0, tiled=True)  339 us
    unnamed x5, waiting for transfers between devices  184 us
    unnamed x1, blocking collectives  37.2 us
    psum x1, blocking collectives, local(): shrunk_group = lax.psum(picked, 'adapter').astype(jnp.bfloat16)  35.4 us
    all_gather x1, blocking collectives, local(): low_group = lax.all_gather(low_rank, 'adapter', axis=0, tiled=True)  20.2 us
    all_to_all x1, local copies, waits for them, and re-layouts, local(): lax.all_to_all(w_down, 'adapter', split_axis=0, concat_axis=1, tiled=True)  19.9 us
  transfers between devices with their start and end apart: 4, of which 2 were waited for; matrix products, arithmetic and copies ran while one was open for 8% of the time, Pallas kernels for 0%

commit v1 on v0

v1 whole, which is shorter than its diff:
```python
import functools

import jax
import jax.numpy as jnp
from jax import lax
from jax.experimental import pallas as pl
from jax.experimental.pallas import tpu as pltpu
from jax.sharding import PartitionSpec as P

R = 16
LANES = 128
CHUNKS = 4
MESH = pl.DeviceIdType.MESH
F32 = jnp.float32
BF16 = jnp.bfloat16


def dot(a, b):
    return jnp.dot(a, b, preferred_element_type=F32)


def iota(shape, axis):
    return lax.broadcasted_iota(jnp.int32, shape, axis)


def kernel(
    nt, na, x_ref, wg_ref, wu_ref, wd_ref, ag_ref, au_ref, bg_ref, bu_ref, ad_ref, bd_ref,
    len_ref, radp_ref, plc_ref, out_ref,
    xbuf, xc, perm, wbuf, wd, ab, bgu, ad, bd, acc, acc_s, shr, spread, hbuf, accd,
    breq, br_recv, br_all, low_src, low_recv, low2, bsrc, brecv, packed,
    wsem, lsem, xs_sem, xr_sem, as_sem, ar_sem, ts_sem, tr_sem, hs_sem, hr_sem,
):
    t, a = lax.axis_index("tensor"), lax.axis_index("adapter")
    tokens = acc_s.shape[0]
    f = ad.shape[0]
    d_model = ab.shape[0]
    df = accd.shape[1]
    kc = xc.shape[2]
    kq = d_model // 4
    n = na * nt
    tg = tokens // nt
    rows_t = br_recv.shape[1]
    slots = LANES // R
    reqs = len_ref.shape[0]

    def adapter_copy(src, dst, kind, j, target):
        return pltpu.make_async_remote_copy(
            src_ref=src, dst_ref=dst, send_sem=as_sem.at[kind, j], recv_sem=ar_sem.at[kind, j],
            device_id=(t, target), device_id_type=MESH)

    def tensor_copy(src, dst, kind, j, target):
        return pltpu.make_async_remote_copy(
            src_ref=src, dst_ref=dst, send_sem=ts_sem.at[kind, j], recv_sem=tr_sem.at[kind, j],
            device_id=(target, a), device_id_type=MESH)

    def w_copies(c):
        got = []
        for q in range(4):
            rows = pl.ds(q * kq + c * kc, kc)
            got.append(pltpu.make_async_copy(
                wg_ref.at[rows, :], wbuf.at[c % 2, q, :, pl.ds(0, f)], wsem.at[c % 2, q, 0]))
            got.append(pltpu.make_async_copy(
                wu_ref.at[rows, :], wbuf.at[c % 2, q, :, pl.ds(f, f)], wsem.at[c % 2, q, 1]))
        return got

    x_own = [pltpu.make_async_copy(
        x_ref.at[:, pl.ds(c * kc, kc)], xbuf.at[c, 0], lsem.at[c]) for c in range(CHUNKS)]
    load_bd = pltpu.make_async_copy(bd_ref, bd, lsem.at[4])
    load_ag = pltpu.make_async_copy(ag_ref, ab.at[:, pl.ds(0, LANES)], lsem.at[5])
    load_au = pltpu.make_async_copy(au_ref, ab.at[:, pl.ds(LANES, LANES)], lsem.at[6])
    load_bg = pltpu.make_async_copy(bg_ref, bgu.at[0], lsem.at[7])
    load_bu = pltpu.make_async_copy(bu_ref, bgu.at[1], lsem.at[8])
    load_ad = pltpu.make_async_copy(ad_ref, ad, lsem.at[9])
    load_wd = pltpu.make_async_copy(wd_ref, wd, lsem.at[10])
    for copy in x_own + [load_bd] + w_copies(0) + [load_ag, load_au] + w_copies(1):
        copy.start()
    for copy in (load_bg, load_bu, load_ad, load_wd):
        copy.start()

    barrier = pltpu.get_barrier_semaphore()
    for j in range(1, na):
        pl.semaphore_signal(barrier, inc=1, device_id=(t, (a + j) % na), device_id_type=MESH)
    for j in range(1, nt):
        pl.semaphore_signal(barrier, inc=1, device_id=((t + j) % nt, a), device_id_type=MESH)
    pl.semaphore_wait(barrier, na + nt - 2)

    steps = []
    bit = na // 2
    while bit:
        steps.append((0, bit))
        bit //= 2
    bit = nt // 2
    while bit:
        steps.append((1, bit))
        bit //= 2

    def flip(v, b):
        return v + b - 2 * b * ((v // b) % 2)

    def x_copy(k, c):
        axis, b = steps[k]
        target = (t, flip(a, b)) if axis == 0 else (flip(t, b), a)
        return pltpu.make_async_remote_copy(
            src_ref=xbuf.at[c, pl.ds(0, 1 << k)], dst_ref=xbuf.at[c, pl.ds(1 << k, 1 << k)],
            send_sem=xs_sem.at[k, c], recv_sem=xr_sem.at[k, c],
            device_id=target, device_id_type=MESH)

    last = len(steps) - 1

    def x_start(k, c):
        if k == 0:
            x_own[c].wait()
        else:
            x_copy(k - 1, c).wait_recv()
        x_copy(k, c).start()

    for wave in range(CHUNKS + last - 1):
        for k in range(last):
            if 0 <= wave - k < CHUNKS:
                x_start(k, wave - k)

    def tables(rows, first):
        position = iota((rows, LANES), 0) + first
        adapter = jnp.zeros((rows, LANES), jnp.int32)
        slot = jnp.zeros((rows, LANES), jnp.int32)
        request = jnp.zeros((rows, LANES), jnp.int32)
        start = 0
        for r in range(reqs):
            end = start + len_ref[r]
            inside = (position >= start) & (position < end)
            adapter = jnp.where(inside, radp_ref[r], adapter)
            slot = jnp.where(inside, plc_ref[radp_ref[r]], slot)
            request = jnp.where(inside, r, request)
            start = end
        return adapter, slot, request

    row, col = iota((LANES, LANES), 0), iota((LANES, LANES), 1)
    slot_of_row = jnp.full((LANES, LANES), -1, jnp.int32)
    for r in range(reqs):
        slot_of_row = jnp.where(row // R == r, plc_ref[radp_ref[r]], slot_of_row)
    choose = (slot_of_row == a * slots + col // R) & (row % R == col % R)
    choose = jnp.where(choose, 1.0, 0.0).astype(BF16)
    load_bd.wait()

    def choose_block(i, carry):
        off = pl.multiple_of(i * df, LANES)
        breq[i] = dot(choose, bd[:, pl.ds(off, df)]).astype(BF16)
        return carry

    lax.fori_loop(0, na, choose_block, 0)
    own_rows = pl.ds(pl.multiple_of(t * rows_t, rows_t), rows_t)

    def br_copy(j):
        target = (a + j) % na
        return adapter_copy(breq.at[target, own_rows], br_recv.at[j], 0, j, target)

    for j in range(1, na):
        br_copy(j).start()
    br_recv[0] = breq[a, own_rows]

    def perm_block(q, carry):
        p_row, p_col = iota((tokens, n * 16), 0), iota((tokens, n * 16), 1)
        s, i, pq = p_col // 16, (p_col % 16) // 4, p_col % 4
        src_t, src_a = jnp.full_like(s, t), jnp.full_like(s, a)
        for k, (axis, b) in enumerate(steps):
            on = ((s // (1 << k)) % 2) == 1
            if axis == 0:
                src_a = jnp.where(on, src_a + (b - 2 * b * ((a // b) % 2)), src_a)
            else:
                src_t = jnp.where(on, src_t + (b - 2 * b * ((t // b) % 2)), src_t)
        hit = (p_row == (src_t * na + src_a) * 4 + i) & (pq == q)
        perm[q] = jnp.where(hit, 1.0, 0.0).astype(BF16)
        return carry

    lax.fori_loop(0, 4, perm_block, 0)
    adapter_t, slot_t, _ = tables(tokens, 0)

    tile = 256 if (2 * f) % 256 == 0 else LANES
    x_start(last, 0)
    for c in range(CHUNKS):
        if c + 1 < CHUNKS:
            x_start(last, c + 1)
        x_copy(last, c).wait_recv()

        def arrange(q, carry):
            block = xbuf[c].reshape(n * 16, kc)
            xc[q] = dot(perm[q], block).astype(BF16)
            return carry

        lax.fori_loop(0, 4, arrange, 0)
        if c == 0:
            load_ag.wait()
            load_au.wait()
        part = dot(xc[0], ab[pl.ds(c * kc, kc), :])
        for q in range(1, 4):
            part += dot(xc[q], ab[pl.ds(q * kq + c * kc, kc), :])
        if c == 0:
            acc_s[...] = part
        else:
            acc_s[...] += part

        if c == CHUNKS - 1:
            total = jnp.zeros((tokens // 4, LANES), F32)
            for h in range(2):
                kept = jnp.where(slot_t == a * slots + iota((tokens, LANES), 1) // R,
                                 acc_s[:, h * LANES:(h + 1) * LANES], 0.0).astype(BF16)
                for g in range(4):
                    to = (col // 32 == g) & ((col % 32) // R == h) & (row % R == col % R)
                    total += dot(kept[g * (tokens // 4):(g + 1) * (tokens // 4)],
                                 jnp.where(to, 1.0, 0.0).astype(BF16))
            shr[0] = total.astype(BF16)
            for j in range(1, na):
                adapter_copy(shr.at[0], shr.at[j], 1, j, (a + j) % na).start()

        for copy in w_copies(c):
            copy.wait()

        def gate_up(i, carry):
            cols = pl.ds(pl.multiple_of(i * tile, tile), tile)
            s = dot(xc[0], wbuf[c % 2, 0, :, cols])
            for q in range(1, 4):
                s += dot(xc[q], wbuf[c % 2, q, :, cols])
            if c == 0:
                acc[:, cols] = s
            else:
                acc[:, cols] += s
            return carry

        lax.fori_loop(0, 2 * f // tile, gate_up, 0)
        if c + 2 < CHUNKS:
            for copy in w_copies(c + 2):
                copy.start()

    for j in range(1, na):
        br_copy(j).wait_recv()
    rows_sum = br_recv[0].astype(F32)
    for j in range(1, na):
        rows_sum += br_recv[j].astype(F32)
    br_all[t] = rows_sum.astype(BF16)
    for j in range(1, nt):
        tensor_copy(br_all.at[t], br_all.at[t], 0, j, (t + j) % nt).start()

    for j in range(1, na):
        adapter_copy(shr.at[0], shr.at[j], 1, j, (a + j) % na).wait_recv()
    shrunk = shr[0].astype(F32)
    for j in range(1, na):
        shrunk += shr[j].astype(F32)
    shrunk = shrunk.astype(BF16)
    load_bg.wait()
    load_bu.wait()
    quarter = tokens // 4
    for h in range(2):
        for g in range(4):
            frm = (row // 32 == g) & ((row % 32) // R == h) & (row % R == col % R)
            value = dot(shrunk, jnp.where(frm, 1.0, 0.0).astype(BF16))
            ids = adapter_t[g * quarter:(g + 1) * quarter]
            lane = iota((quarter, LANES), 1) // R
            for blk in range(spread.shape[2] // LANES):
                spread[h, g * quarter:(g + 1) * quarter, blk * LANES:(blk + 1) * LANES] = jnp.where(
                    ids == blk * slots + lane, value, 0.0).astype(BF16)

    def make_hidden(i, carry):
        cols = pl.ds(pl.multiple_of(i * LANES, LANES), LANES)
        up_cols = pl.ds(pl.multiple_of(f + i * LANES, LANES), LANES)
        gate = acc[:, cols] + dot(spread[0], bgu[0, :, cols])
        up = acc[:, up_cols] + dot(spread[1], bgu[1, :, cols])
        hbuf[0, :, cols] = (gate / (1.0 + jnp.exp(-gate)) * up).astype(BF16)
        return carry

    lax.fori_loop(0, f // LANES, make_hidden, 0)

    half = na // 2
    mate = flip(a, 1)

    def h_copy(j):
        if j < half:
            src, dst, target = hbuf.at[0], hbuf.at[j], (a + 2 * j) % na
        else:
            src, dst, target = hbuf.at[j - half], hbuf.at[j], mate
        return pltpu.make_async_remote_copy(
            src_ref=src, dst_ref=dst, send_sem=hs_sem.at[j], recv_sem=hr_sem.at[j],
            device_id=(t, target), device_id_type=MESH)

    h_copy(half).start()
    for j in range(1, half):
        h_copy(j).start()

    load_ad.wait()

    def low_block(i, carry):
        cols = pl.ds(pl.multiple_of(i * LANES, LANES), LANES)
        value = dot(hbuf[0], ad[:, cols])
        return carry + jnp.where(adapter_t == i * slots + iota((tokens, LANES), 1) // R, value, 0.0)

    low = lax.fori_loop(0, ad.shape[1] // LANES, low_block, jnp.zeros((tokens, LANES), F32))
    same = jnp.where(row % R == col % R, 1.0, 0.0).astype(BF16)
    low = dot(low.astype(BF16), same).astype(BF16)
    for g in range(nt):
        low_src[g] = low[g * tg:(g + 1) * tg]

    def low_copy(j):
        return tensor_copy(low_src.at[(t + j) % nt], low_recv.at[j], 1, j, (t + j) % nt)

    for j in range(1, nt):
        low_copy(j).start()
    low_recv[0] = low_src[t]
    for j in range(1, nt):
        low_copy(j).wait_recv()
    low_sum = low_recv[0].astype(F32)
    for j in range(1, nt):
        low_sum += low_recv[j].astype(F32)
    low2[0] = low_sum.astype(BF16)
    for j in range(1, na):
        adapter_copy(low2.at[0], low2.at[j], 2, j, (a + j) % na).start()

    load_wd.wait()

    dtile = 256 if df % 256 == 0 else LANES

    def down(j, source, first):
        def body(i, carry):
            cols = pl.ds(pl.multiple_of(i * dtile, dtile), dtile)
            value = dot(hbuf[j], wd[source, :, cols])
            if first:
                accd[:, cols] = value
            else:
                accd[:, cols] += value
            return carry

        lax.fori_loop(0, df // dtile, body, 0)

    down(0, a, True)
    for j in range(1, half):
        h_copy(j).wait_recv()
        h_copy(half + j).start()
        down(j, (a + na - 2 * j) % na, False)
    for j in range(half):
        h_copy(half + j).wait_recv()
        down(half + j, (mate + na - 2 * j) % na, False)

    for g in range(nt):
        bsrc[g] = accd[g * tg:(g + 1) * tg].astype(BF16)

    def base_copy(j):
        return tensor_copy(bsrc.at[(t + j) % nt], brecv.at[j], 2, j, (t + j) % nt)

    for j in range(1, nt):
        base_copy(j).start()
    brecv[0] = bsrc[t]

    for j in range(1, na):
        adapter_copy(low2.at[0], low2.at[j], 2, j, (a + j) % na).wait_recv()
    low_all = low2[0].astype(F32)
    for j in range(1, na):
        low_all += low2[j].astype(F32)
    _, _, request_g = tables(tg, t * tg)
    low_all = jnp.where(request_g == iota((tg, LANES), 1) // R, low_all, 0.0).astype(BF16)
    for j in range(1, nt):
        other = (t + nt - j) % nt
        tensor_copy(br_all.at[other], br_all.at[other], 0, j, (t + j) % nt).wait_recv()
    delta = dot(low_all, br_all[...].reshape(nt * rows_t, df)).astype(BF16).astype(F32)

    for j in range(1, nt):
        base_copy(j).wait_recv()
    base = brecv[0].astype(F32)
    for j in range(1, nt):
        base += brecv[j].astype(F32)
    mixed = (base + delta).astype(BF16)

    fq = df // 4
    o_row, o_col = iota((na * 16, tg), 0), iota((na * 16, tg), 1)
    result = jnp.zeros((na * 16, fq), F32)
    for q in range(4):
        hit = ((o_row % 16) // 4 == q) & (o_col == (o_row // 16) * 4 + o_row % 4)
        result += dot(jnp.where(hit, 1.0, 0.0).astype(BF16), mixed[:, q * fq:(q + 1) * fq])
    packed[...] = result.astype(BF16).reshape(na, 16, fq)

    def out_copy(j):
        target = (a + j) % na
        return adapter_copy(packed.at[target], out_ref.at[a], 3, j, target)

    for j in range(1, na):
        out_copy(j).start()
    out_ref[a] = packed[a]
    for j in range(1, na):
        other = (a + na - j) % na
        adapter_copy(packed.at[other], out_ref.at[other], 3, j, other).wait_recv()

    for k in range(len(steps)):
        for c in range(CHUNKS):
            x_copy(k, c).wait_send()
    for j in range(1, na):
        br_copy(j).wait_send()
        adapter_copy(shr.at[0], shr.at[j], 1, j, (a + j) % na).wait_send()
        adapter_copy(low2.at[0], low2.at[j], 2, j, (a + j) % na).wait_send()
        out_copy(j).wait_send()
        h_copy(j).wait_send()
    for j in range(1, nt):
        tensor_copy(br_all.at[t], br_all.at[t], 0, j, (t + j) % nt).wait_send()
        low_copy(j).wait_send()
        base_copy(j).wait_send()


def local(nt, na, x, w_gate, w_up, w_down, a_gate, a_up, b_gate, b_up, a_down, b_down,
          lengths, request_adapter, placement):
    tok, d_model = x.shape
    tokens = tok * nt * na
    f0 = w_gate.shape[1]
    f = -(-f0 // LANES) * LANES
    df = w_down.shape[1]
    w_down = w_down.reshape(na, f0, df)
    if f != f0:
        wide = ((0, 0), (0, f - f0))
        w_gate, w_up = jnp.pad(w_gate, wide), jnp.pad(w_up, wide)
        b_gate, b_up = jnp.pad(b_gate, wide), jnp.pad(b_up, wide)
        a_down = jnp.pad(a_down, ((0, f - f0), (0, 0)))
        w_down = jnp.pad(w_down, ((0, 0), (0, f - f0), (0, 0)))
    x = x.reshape(tok * 4, d_model // 4)
    n = nt * na
    kc = d_model // 4 // CHUNKS
    ranks = b_gate.shape[0]
    rows_t = LANES // nt
    tg = tokens // nt
    nsteps = n.bit_length() - 1
    anyspace = pl.BlockSpec(memory_space=pl.ANY)
    smem = pl.BlockSpec(memory_space=pltpu.SMEM)
    dma = pltpu.SemaphoreType.DMA
    out = pl.pallas_call(
        functools.partial(kernel, nt, na),
        out_shape=jax.ShapeDtypeStruct((na, 16, df // 4), BF16),
        in_specs=[anyspace] * 10 + [smem] * 3,
        out_specs=pl.BlockSpec(memory_space=pltpu.VMEM),
        scratch_shapes=[
            pltpu.VMEM((CHUNKS, n, 16, kc), BF16),
            pltpu.VMEM((4, tokens, kc), BF16),
            pltpu.VMEM((4, tokens, n * 16), BF16),
            pltpu.VMEM((2, 4, kc, 2 * f), BF16),
            pltpu.VMEM((na, f, df), BF16),
            pltpu.VMEM((d_model, 2 * LANES), BF16),
            pltpu.VMEM((2, ranks, f), BF16),
            pltpu.VMEM((f, ranks), BF16),
            pltpu.VMEM((LANES, b_down.shape[1]), BF16),
            pltpu.VMEM((tokens, 2 * f), F32),
            pltpu.VMEM((tokens, 2 * LANES), F32),
            pltpu.VMEM((na, tokens // 4, LANES), BF16),
            pltpu.VMEM((2, tokens, ranks), BF16),
            pltpu.VMEM((na, tokens, f), BF16),
            pltpu.VMEM((tokens, df), F32),
            pltpu.VMEM((na, LANES, df), BF16),
            pltpu.VMEM((na, rows_t, df), BF16),
            pltpu.VMEM((nt, rows_t, df), BF16),
            pltpu.VMEM((nt, tg, LANES), BF16),
            pltpu.VMEM((nt, tg, LANES), BF16),
            pltpu.VMEM((na, tg, LANES), BF16),
            pltpu.VMEM((nt, tg, df), BF16),
            pltpu.VMEM((nt, tg, df), BF16),
            pltpu.VMEM((na, 16, df // 4), BF16),
            dma((2, 4, 2)),
            dma((11,)),
            dma((nsteps, CHUNKS)),
            dma((nsteps, CHUNKS)),
            dma((4, na)),
            dma((4, na)),
            dma((3, nt)),
            dma((3, nt)),
            dma((na,)),
            dma((na,)),
        ],
        compiler_params=pltpu.CompilerParams(
            collective_id=0, has_side_effects=True, vmem_limit_bytes=60 * 1024 * 1024),
    )(x, w_gate, w_up, w_down, a_gate, a_up, b_gate, b_up, a_down, b_down,
      lengths, request_adapter, placement)
    out = out.reshape(na, 4, tok, df // 4).transpose(2, 0, 1, 3)
    return out.reshape(tok, na * df)


def solution(mesh):
    nt, na = mesh.shape["tensor"], mesh.shape["adapter"]
    both = ("tensor", "adapter")
    in_specs = (
        P(both, None),
        P(None, both),
        P(None, both),
        P("tensor", "adapter"),
        P(None, "adapter"),
        P(None, "adapter"),
        P(None, both),
        P(None, both),
        P(both, None),
        P("adapter", None),
        P(),
        P(),
        P(),
    )
    return jax.shard_map(
        functools.partial(local, nt, na), mesh=mesh, in_specs=in_specs,
        out_specs=P(both, None), check_vma=False)
```

time: 704 us -> 93.4 us (0.13)
  blocking collectives: 437 us -> 0 us
  waiting for transfers between devices: 184 us -> 0 us
  Pallas kernels: 0 us -> 90.2 us
  matrix products: 33.8 us -> 0 us
  local copies, waits for them, and re-layouts: 24.8 us -> 3 us
  between operations: 14 us -> 0.01 us
  starting transfers between devices: 7.69 us -> 0 us
    all_gather x3 -> x0, blocking collectives: 364 us -> none  [the longest x1 339 us: local(): rows_group = lax.all_gather(tokens_in, 'adapter', axis=0, tiled=True)]
    unnamed x5 -> x0, waiting for transfers between devices: 184 us -> none
    pallas_call x0 -> x1, Pallas kernels: none -> 90.2 us  [local(): pl.pallas_call(functools.partial(kernel, nt, na), out_shape=jax.ShapeDtyp...]
    unnamed x1 -> x0, blocking collectives: 37.2 us -> none
    psum x1 -> x0, blocking collectives: 35.4 us -> none  [local(): shrunk_group = lax.psum(picked, 'adapter').astype(jnp.bfloat16)]
    dot_general x9 -> x0, matrix products: 33.8 us -> none  [the longest x1 11.9 us: local(): base_part = jnp.dot(hidden, down_full, preferred_element_type=jnp.float32)]
    all_to_all x1 -> x0, local copies, waits for them, and re-layouts: 19.9 us -> none  [local(): lax.all_to_all(w_down, 'adapter', split_axis=0, concat_axis=1, tiled=True)]
    all_to_all x1 -> x0, starting transfers between devices: 7.38 us -> none  [local(): lax.all_to_all(w_down, 'adapter', split_axis=0, concat_axis=1, tiled=True)]
  transfers between devices with their start and end apart: 4 -> 0, of which waited for: 2 -> 0; matrix products, arithmetic and copies ran while one was open for 8% -> 0% of each run, Pallas kernels for 0% -> 0%
where the time goes in v1:
time: 93.4 us; the launch traced here: 93.2 us
  Pallas kernels  90.2 us (97%)
  local copies, waits for them, and re-layouts  3 us (3%)
    pallas_call x1, Pallas kernels, local(): pl.pallas_call(functools.partial(kernel, nt, na), out_shape=jax.ShapeDtyp...  90.2 us

profile of v1, /device:TPU:0, one launch (start us, length us, event | category | flops | bytes accessed | tf_op | source)
XLA Modules:
  0.0 93.2 jit_solution(15670001288580210081)
XLA Ops:
  0.0 1.5 %reshape.12.x_ref = bf16[16,2048]{1,0:T(8,128)(2,1)} reshape(bf16[4,8192]{1,0:T(4,128)(2,1)} %param.13) | data formatting | bytes 131072 | tf_op jit(solution)/shard_map/reshape | solution.py:418
  1.5 90.2 %shard_map.127 = bf16[8,16,256]{2,1,0:T(8,128)(2,1)} custom-call(bf16[16,2048]{1,0:T(8,128)(2,1)} %reshape.12.x_ref, bf16[8192,896]{1,0:T(8,128)(2,1)} %wg_ref.1, bf16[8192,896]{1,0:T(8,128)(2,1)} %wu_ref.1, bf16[8,896,1024]{2,1,0:T(8,128)(2,1)} %bitcast.4, bf16[8192,128]{1,0:T(8,128)(2,1)} %ag_ref.1, bf16[8192,128]{1,0:T(8,128)(2,1)} %au_ref.1, ...), custom_call_target="tpu_custom_call" | custom-call | tf_op jit(solution)/shard_map/pallas_call | solution.py:428
  91.7 1.5 %reshape.14 = bf16[8,4,4,256]{3,2,1,0:T(4,128)(2,1)} reshape(bf16[8,16,256]{2,1,0:T(8,128)(2,1)} %shard_map.127) | data formatting | bytes 131072 | tf_op jit(solution)/shard_map/reshape | solution.py:473

commit v2 on v1

--- a/solution.py
+++ b/solution.py
@@ -24,9 +24,9 @@
 
 
 def kernel(
-    nt, na, x_ref, wg_ref, wu_ref, wd_ref, ag_ref, au_ref, bg_ref, bu_ref, ad_ref, bd_ref,
+    nt, na, pieces, x_ref, wg_ref, wu_ref, wd_ref, ag_ref, au_ref, bg_ref, bu_ref, ad_ref, bd_ref,
     len_ref, radp_ref, plc_ref, out_ref,
-    xbuf, xc, perm, wbuf, wd, ab, bgu, ad, bd, acc, acc_s, shr, spread, hbuf, accd,
+    xbuf, xc, split, canon, wbuf, wd, ab, bgu, bsel, ad, bd, acc, acc_s, shr, spread, hbuf, accd,
     breq, br_recv, br_all, low_src, low_recv, low2, bsrc, brecv, packed,
     wsem, lsem, xs_sem, xr_sem, as_sem, ar_sem, ts_sem, tr_sem, hs_sem, hr_sem,
 ):
@@ -35,7 +35,7 @@
     f = ad.shape[0]
     d_model = ab.shape[0]
     df = accd.shape[1]
-    kc = xc.shape[2]
+    kc = xc.shape[3]
     kq = d_model // 4
     n = na * nt
     tg = tokens // nt
@@ -158,9 +158,12 @@
         br_copy(j).start()
     br_recv[0] = breq[a, own_rows]
 
-    def perm_block(q, carry):
-        p_row, p_col = iota((tokens, n * 16), 0), iota((tokens, n * 16), 1)
-        s, i, pq = p_col // 16, (p_col % 16) // 4, p_col % 4
+    s_row, s_col = iota((256, 256), 0), iota((256, 256), 1)
+    hit = (s_row // 64 == s_col % 4) & (s_row % 64 == s_col // 4)
+    split[...] = jnp.where(hit, 1.0, 0.0).astype(BF16)
+
+    def owner_row(place):
+        s = place // 4
         src_t, src_a = jnp.full_like(s, t), jnp.full_like(s, a)
         for k, (axis, b) in enumerate(steps):
             on = ((s // (1 << k)) % 2) == 1
@@ -168,69 +171,137 @@
                 src_a = jnp.where(on, src_a + (b - 2 * b * ((a // b) % 2)), src_a)
             else:
                 src_t = jnp.where(on, src_t + (b - 2 * b * ((t // b) % 2)), src_t)
-        hit = (p_row == (src_t * na + src_a) * 4 + i) & (pq == q)
-        perm[q] = jnp.where(hit, 1.0, 0.0).astype(BF16)
-        return carry
-
-    lax.fori_loop(0, 4, perm_block, 0)
-    adapter_t, slot_t, _ = tables(tokens, 0)
-
-    tile = 256 if (2 * f) % 256 == 0 else LANES
-    x_start(last, 0)
-    for c in range(CHUNKS):
+        return (src_t * na + src_a) * 4 + place % 4
+
+    c_row, c_col = iota((tokens, tokens), 0), iota((tokens, tokens), 1)
+    canon[0] = jnp.where(c_row == owner_row(c_col), 1.0, 0.0).astype(BF16)
+    canon[1] = jnp.where(c_col == owner_row(c_row), 1.0, 0.0).astype(BF16)
+    adapter_t, slot_t, request_t = tables(tokens, 0)
+
+    tile = 256
+    quarter = tokens // 4
+
+    def arrive(c):
         if c + 1 < CHUNKS:
             x_start(last, c + 1)
         x_copy(last, c).wait_recv()
 
-        def arrange(q, carry):
-            block = xbuf[c].reshape(n * 16, kc)
-            xc[q] = dot(perm[q], block).astype(BF16)
+        def arrange(g, carry):
+            block = xbuf[c, pl.ds(g * 16, 16)].reshape(256, kc)
+            value = dot(split[...], block).astype(BF16)
+            for q in range(4):
+                xc[c % 2, q, pl.ds(pl.multiple_of(g * 64, 64), 64)] = value[q * 64:(q + 1) * 64]
             return carry
 
-        lax.fori_loop(0, 4, arrange, 0)
+        lax.fori_loop(0, n // 16, arrange, 0)
         if c == 0:
             load_ag.wait()
             load_au.wait()
-        part = dot(xc[0], ab[pl.ds(c * kc, kc), :])
+        part = dot(xc[c % 2, 0], ab[pl.ds(c * kc, kc), :])
         for q in range(1, 4):
-            part += dot(xc[q], ab[pl.ds(q * kq + c * kc, kc), :])
+            part += dot(xc[c % 2, q], ab[pl.ds(q * kq + c * kc, kc), :])
         if c == 0:
             acc_s[...] = part
         else:
             acc_s[...] += part
 
-        if c == CHUNKS - 1:
-            total = jnp.zeros((tokens // 4, LANES), F32)
-            for h in range(2):
-                kept = jnp.where(slot_t == a * slots + iota((tokens, LANES), 1) // R,
-                                 acc_s[:, h * LANES:(h + 1) * LANES], 0.0).astype(BF16)
-                for g in range(4):
-                    to = (col // 32 == g) & ((col % 32) // R == h) & (row % R == col % R)
-                    total += dot(kept[g * (tokens // 4):(g + 1) * (tokens // 4)],
-                                 jnp.where(to, 1.0, 0.0).astype(BF16))
-            shr[0] = total.astype(BF16)
-            for j in range(1, na):
-                adapter_copy(shr.at[0], shr.at[j], 1, j, (a + j) % na).start()
-
+    def gate_up(c, i):
+        cols = pl.ds(pl.multiple_of(i * tile, tile), tile)
+        s = dot(xc[c % 2, 0], wbuf[c % 2, 0, :, cols])
+        for q in range(1, 4):
+            s += dot(xc[c % 2, q], wbuf[c % 2, q, :, cols])
+        if c == 0:
+            acc[:, cols] = s
+        else:
+            acc[:, cols] += s
+
+    def whole_chunk(c):
         for copy in w_copies(c):
             copy.wait()
 
-        def gate_up(i, carry):
-            cols = pl.ds(pl.multiple_of(i * tile, tile), tile)
-            s = dot(xc[0], wbuf[c % 2, 0, :, cols])
-            for q in range(1, 4):
-                s += dot(xc[q], wbuf[c % 2, q, :, cols])
-            if c == 0:
-                acc[:, cols] = s
-            else:
-                acc[:, cols] += s
+        def body(i, carry):
+            gate_up(c, i)
             return carry
 
-        lax.fori_loop(0, 2 * f // tile, gate_up, 0)
+        lax.fori_loop(0, 2 * f // tile, body, 0)
         if c + 2 < CHUNKS:
             for copy in w_copies(c + 2):
                 copy.start()
 
+    x_start(last, 0)
+    for c in range(CHUNKS - 2):
+        arrive(c)
+        whole_chunk(c)
+    arrive(CHUNKS - 2)
+    arrive(CHUNKS - 1)
+
+    ordered = dot(canon[0], acc_s[...].astype(BF16))
+    total = jnp.zeros((quarter, LANES), F32)
+    for h in range(2):
+        kept = jnp.where(slot_t == a * slots + iota((tokens, LANES), 1) // R,
+                         ordered[:, h * LANES:(h + 1) * LANES], 0.0).astype(BF16)
+        for g in range(4):
+            to = (col // 32 == g) & ((col % 32) // R == h) & (row % R == col % R)
+            total += dot(kept[g * quarter:(g + 1) * quarter],
+                         jnp.where(to, 1.0, 0.0).astype(BF16))
+    shr[0] = total.astype(BF16)
+    for j in range(1, na):
+        adapter_copy(shr.at[0], shr.at[j], 1, j, (a + j) % na).start()
+
+    whole_chunk(CHUNKS - 2)
+
+    load_bg.wait()
+    load_bu.wait()
+    for r in range(reqs):
+        for h in range(2):
+            bsel[h, r * R:(r + 1) * R] = bgu[h, radp_ref[r]]
+    for j in range(1, na):
+        adapter_copy(shr.at[0], shr.at[j], 1, j, (a + j) % na).wait_recv()
+    shrunk = shr[0].astype(F32)
+    for j in range(1, na):
+        shrunk += shr[j].astype(F32)
+    shrunk = shrunk.astype(BF16)
+    for h in range(2):
+        parts = []
+        for g in range(4):
+            frm = (row // 32 == g) & ((row % 32) // R == h) & (row % R == col % R)
+            parts.append(dot(shrunk, jnp.where(frm, 1.0, 0.0).astype(BF16)))
+        value = jnp.concatenate(parts, axis=0)
+        value = jnp.where(request_t == iota((tokens, LANES), 1) // R, value, 0.0).astype(BF16)
+        spread[h] = dot(canon[1], value).astype(BF16)
+
+    half = na // 2
+    mate = flip(a, 1)
+
+    def h_copy(p, j):
+        cols = pl.ds(pieces[p][0], pieces[p][1] - pieces[p][0])
+        frm = 0 if j < half else j - half
+        target = (a + 2 * j) % na if j < half else mate
+        return pltpu.make_async_remote_copy(
+            src_ref=hbuf.at[frm, :, cols], dst_ref=hbuf.at[j, :, cols],
+            send_sem=hs_sem.at[p, j], recv_sem=hr_sem.at[p, j],
+            device_id=(t, target), device_id_type=MESH)
+
+    for copy in w_copies(CHUNKS - 1):
+        copy.wait()
+    full, odd = f // 256, (f // LANES) % 2
+    for p, (lo, hi) in enumerate(pieces):
+        tiles = [p] if p < full else []
+        if odd and p == 0:
+            tiles.append(full)
+        if p < full:
+            tiles.append(full + odd + p)
+        for i in tiles:
+            gate_up(CHUNKS - 1, i)
+        for c0 in range(lo, hi, LANES):
+            gate = acc[:, c0:c0 + LANES] + dot(spread[0], bsel[0, :, c0:c0 + LANES])
+            up = acc[:, f + c0:f + c0 + LANES] + dot(spread[1], bsel[1, :, c0:c0 + LANES])
+            value = (gate / (1.0 + jnp.exp(-gate)) * up).astype(BF16)
+            hbuf[0, :, c0:c0 + LANES] = dot(canon[0], value).astype(BF16)
+        h_copy(p, half).start()
+        for j in range(1, half):
+            h_copy(p, j).start()
+
     for j in range(1, na):
         br_copy(j).wait_recv()
     rows_sum = br_recv[0].astype(F32)
@@ -240,59 +311,17 @@
     for j in range(1, nt):
         tensor_copy(br_all.at[t], br_all.at[t], 0, j, (t + j) % nt).start()
 
-    for j in range(1, na):
-        adapter_copy(shr.at[0], shr.at[j], 1, j, (a + j) % na).wait_recv()
-    shrunk = shr[0].astype(F32)
-    for j in range(1, na):
-        shrunk += shr[j].astype(F32)
-    shrunk = shrunk.astype(BF16)
-    load_bg.wait()
-    load_bu.wait()
-    quarter = tokens // 4
-    for h in range(2):
-        for g in range(4):
-            frm = (row // 32 == g) & ((row % 32) // R == h) & (row % R == col % R)
-            value = dot(shrunk, jnp.where(frm, 1.0, 0.0).astype(BF16))
-            ids = adapter_t[g * quarter:(g + 1) * quarter]
-            lane = iota((quarter, LANES), 1) // R
-            for blk in range(spread.shape[2] // LANES):
-                spread[h, g * quarter:(g + 1) * quarter, blk * LANES:(blk + 1) * LANES] = jnp.where(
-                    ids == blk * slots + lane, value, 0.0).astype(BF16)
-
-    def make_hidden(i, carry):
-        cols = pl.ds(pl.multiple_of(i * LANES, LANES), LANES)
-        up_cols = pl.ds(pl.multiple_of(f + i * LANES, LANES), LANES)
-        gate = acc[:, cols] + dot(spread[0], bgu[0, :, cols])
-        up = acc[:, up_cols] + dot(spread[1], bgu[1, :, cols])
-        hbuf[0, :, cols] = (gate / (1.0 + jnp.exp(-gate)) * up).astype(BF16)
+    load_ad.wait()
+
+    def low_block(i, carry):
+        cols = pl.ds(pl.multiple_of(i * 256, 256), 256)
+        value = dot(hbuf[0], ad[:, cols])
+        for h in range(2):
+            owner = (2 * i + h) * slots + iota((tokens, LANES), 1) // R
+            carry += jnp.where(adapter_t == owner, value[:, h * LANES:(h + 1) * LANES], 0.0)
         return carry
 
-    lax.fori_loop(0, f // LANES, make_hidden, 0)
-
-    half = na // 2
-    mate = flip(a, 1)
-
-    def h_copy(j):
-        if j < half:
-            src, dst, target = hbuf.at[0], hbuf.at[j], (a + 2 * j) % na
-        else:
-            src, dst, target = hbuf.at[j - half], hbuf.at[j], mate
-        return pltpu.make_async_remote_copy(
-            src_ref=src, dst_ref=dst, send_sem=hs_sem.at[j], recv_sem=hr_sem.at[j],
-            device_id=(t, target), device_id_type=MESH)
-
-    h_copy(half).start()
-    for j in range(1, half):
-        h_copy(j).start()
-
-    load_ad.wait()
-
-    def low_block(i, carry):
-        cols = pl.ds(pl.multiple_of(i * LANES, LANES), LANES)
-        value = dot(hbuf[0], ad[:, cols])
-        return carry + jnp.where(adapter_t == i * slots + iota((tokens, LANES), 1) // R, value, 0.0)
-
-    low = lax.fori_loop(0, ad.shape[1] // LANES, low_block, jnp.zeros((tokens, LANES), F32))
+    low = lax.fori_loop(0, ad.shape[1] // 256, low_block, jnp.zeros((tokens, LANES), F32))
     same = jnp.where(row % R == col % R, 1.0, 0.0).astype(BF16)
     low = dot(low.astype(BF16), same).astype(BF16)
     for g in range(nt):
@@ -317,10 +346,12 @@
 
     dtile = 256 if df % 256 == 0 else LANES
 
-    def down(j, source, first):
+    def down(p, j, source, first=False):
+        lo, hi = pieces[p]
+
         def body(i, carry):
             cols = pl.ds(pl.multiple_of(i * dtile, dtile), dtile)
-            value = dot(hbuf[j], wd[source, :, cols])
+            value = dot(hbuf[j, :, lo:hi], wd[source, lo:hi, cols])
             if first:
                 accd[:, cols] = value
             else:
@@ -329,14 +360,17 @@
 
         lax.fori_loop(0, df // dtile, body, 0)
 
-    down(0, a, True)
-    for j in range(1, half):
-        h_copy(j).wait_recv()
-        h_copy(half + j).start()
-        down(j, (a + na - 2 * j) % na, False)
-    for j in range(half):
-        h_copy(half + j).wait_recv()
-        down(half + j, (mate + na - 2 * j) % na, False)
+    for p in range(len(pieces)):
+        for j in range(1, half):
+            h_copy(p, j).wait_recv()
+            h_copy(p, half + j).start()
+        down(p, 0, a, p == 0)
+        for j in range(1, half):
+            down(p, j, (a + na - 2 * j) % na)
+    for p in range(len(pieces)):
+        for j in range(half):
+            h_copy(p, half + j).wait_recv()
+            down(p, half + j, (mate + na - 2 * j) % na)
 
     for g in range(nt):
         bsrc[g] = accd[g * tg:(g + 1) * tg].astype(BF16)
@@ -394,7 +428,8 @@
         adapter_copy(shr.at[0], shr.at[j], 1, j, (a + j) % na).wait_send()
         adapter_copy(low2.at[0], low2.at[j], 2, j, (a + j) % na).wait_send()
         out_copy(j).wait_send()
-        h_copy(j).wait_send()
+        for p in range(len(pieces)):
+            h_copy(p, j).wait_send()
     for j in range(1, nt):
         tensor_copy(br_all.at[t], br_all.at[t], 0, j, (t + j) % nt).wait_send()
         low_copy(j).wait_send()
@@ -416,9 +451,12 @@
         a_down = jnp.pad(a_down, ((0, f - f0), (0, 0)))
         w_down = jnp.pad(w_down, ((0, 0), (0, f - f0), (0, 0)))
     x = x.reshape(tok * 4, d_model // 4)
+    b_gate, b_up = b_gate.reshape(-1, R, f), b_up.reshape(-1, R, f)
+    starts = [256 * p for p in range(max(f // 256, 1))]
+    pieces = tuple(zip(starts, starts[1:] + [f]))
     n = nt * na
     kc = d_model // 4 // CHUNKS
-    ranks = b_gate.shape[0]
+    ranks = a_down.shape[1]
     rows_t = LANES // nt
     tg = tokens // nt
     nsteps = n.bit_length() - 1
@@ -426,24 +464,26 @@
     smem = pl.BlockSpec(memory_space=pltpu.SMEM)
     dma = pltpu.SemaphoreType.DMA
     out = pl.pallas_call(
-        functools.partial(kernel, nt, na),
+        functools.partial(kernel, nt, na, pieces),
         out_shape=jax.ShapeDtypeStruct((na, 16, df // 4), BF16),
         in_specs=[anyspace] * 10 + [smem] * 3,
         out_specs=pl.BlockSpec(memory_space=pltpu.VMEM),
         scratch_shapes=[
             pltpu.VMEM((CHUNKS, n, 16, kc), BF16),
-            pltpu.VMEM((4, tokens, kc), BF16),
-            pltpu.VMEM((4, tokens, n * 16), BF16),
+            pltpu.VMEM((2, 4, tokens, kc), BF16),
+            pltpu.VMEM((256, 256), BF16),
+            pltpu.VMEM((2, tokens, tokens), BF16),
             pltpu.VMEM((2, 4, kc, 2 * f), BF16),
             pltpu.VMEM((na, f, df), BF16),
             pltpu.VMEM((d_model, 2 * LANES), BF16),
-            pltpu.VMEM((2, ranks, f), BF16),
+            pltpu.VMEM((2, ranks // R, R, f), BF16),
+            pltpu.VMEM((2, LANES, f), BF16),
             pltpu.VMEM((f, ranks), BF16),
             pltpu.VMEM((LANES, b_down.shape[1]), BF16),
             pltpu.VMEM((tokens, 2 * f), F32),
             pltpu.VMEM((tokens, 2 * LANES), F32),
             pltpu.VMEM((na, tokens // 4, LANES), BF16),
-            pltpu.VMEM((2, tokens, ranks), BF16),
+            pltpu.VMEM((2, tokens, LANES), BF16),
             pltpu.VMEM((na, tokens, f), BF16),
             pltpu.VMEM((tokens, df), F32),
             pltpu.VMEM((na, LANES, df), BF16),
@@ -463,8 +503,8 @@
             dma((4, na)),
             dma((3, nt)),
             dma((3, nt)),
-            dma((na,)),
-            dma((na,)),
+            dma((len(pieces), na)),
+            dma((len(pieces), na)),
         ],
         compiler_params=pltpu.CompilerParams(
             collective_id=0, has_side_effects=True, vmem_limit_bytes=60 * 1024 * 1024),

time: 93.4 us -> 88 us (0.942)
  Pallas kernels: 90.2 us -> 84.8 us
    pallas_call x1, Pallas kernels: 90.2 us -> 84.8 us  [local(): pl.pallas_call(functools.partial(kernel, nt, na, pieces), out_shape=jax.S...]
where the time goes in v2:
time: 88 us; the launch traced here: 87.8 us
  Pallas kernels  84.8 us (96%)
  local copies, waits for them, and re-layouts  3 us (3%)
    pallas_call x1, Pallas kernels, local(): pl.pallas_call(functools.partial(kernel, nt, na, pieces), out_shape=jax.S...  84.8 us

profile of v2, /device:TPU:0, one launch (start us, length us, event | category | flops | bytes accessed | tf_op | source)
XLA Modules:
  0.0 87.8 jit_solution(16392844853208306229)
XLA Ops:
  0.0 1.5 %reshape.18.x_ref = bf16[16,2048]{1,0:T(8,128)(2,1)} reshape(bf16[4,8192]{1,0:T(4,128)(2,1)} %param.13) | data formatting | bytes 131072 | tf_op jit(solution)/shard_map/reshape | solution.py:453
  1.5 84.8 %shard_map.127 = bf16[8,16,256]{2,1,0:T(8,128)(2,1)} custom-call(bf16[16,2048]{1,0:T(8,128)(2,1)} %reshape.18.x_ref, bf16[8192,896]{1,0:T(8,128)(2,1)} %wg_ref.1, bf16[8192,896]{1,0:T(8,128)(2,1)} %wu_ref.1, bf16[8,896,1024]{2,1,0:T(8,128)(2,1)} %bitcast.6, bf16[8192,128]{1,0:T(8,128)(2,1)} %ag_ref.1, bf16[8192,128]{1,0:T(8,128)(2,1)} %au_ref.1, ...), custom_call_target="tpu_custom_call" | custom-call | tf_op jit(solution)/shard_map/pallas_call | solution.py:466
  86.3 1.5 %reshape.22 = bf16[8,4,4,256]{3,2,1,0:T(4,128)(2,1)} reshape(bf16[8,16,256]{2,1,0:T(8,128)(2,1)} %shard_map.127) | data formatting | bytes 131072 | tf_op jit(solution)/shard_map/reshape | solution.py:513

commit v3 on v2

--- a/solution.py
+++ b/solution.py
@@ -35,7 +35,7 @@
     f = ad.shape[0]
     d_model = ab.shape[0]
     df = accd.shape[1]
-    kc = xc.shape[3]
+    kc = xc.shape[2] // 4
     kq = d_model // 4
     n = na * nt
     tg = tokens // nt
@@ -58,9 +58,9 @@
         for q in range(4):
             rows = pl.ds(q * kq + c * kc, kc)
             got.append(pltpu.make_async_copy(
-                wg_ref.at[rows, :], wbuf.at[c % 2, q, :, pl.ds(0, f)], wsem.at[c % 2, q, 0]))
+                wg_ref.at[rows, :], wbuf.at[c % 2, pl.ds(q * kc, kc), pl.ds(0, f)], wsem.at[c % 2, q, 0]))
             got.append(pltpu.make_async_copy(
-                wu_ref.at[rows, :], wbuf.at[c % 2, q, :, pl.ds(f, f)], wsem.at[c % 2, q, 1]))
+                wu_ref.at[rows, :], wbuf.at[c % 2, pl.ds(q * kc, kc), pl.ds(f, f)], wsem.at[c % 2, q, 1]))
         return got
 
     x_own = [pltpu.make_async_copy(
@@ -190,26 +190,24 @@
             block = xbuf[c, pl.ds(g * 16, 16)].reshape(256, kc)
             value = dot(split[...], block).astype(BF16)
             for q in range(4):
-                xc[c % 2, q, pl.ds(pl.multiple_of(g * 64, 64), 64)] = value[q * 64:(q + 1) * 64]
+                xc[c % 2, pl.ds(pl.multiple_of(g * 64, 64), 64), q * kc:(q + 1) * kc] = value[q * 64:(q + 1) * 64]
             return carry
 
         lax.fori_loop(0, n // 16, arrange, 0)
         if c == 0:
             load_ag.wait()
             load_au.wait()
-        part = dot(xc[c % 2, 0], ab[pl.ds(c * kc, kc), :])
+        part = dot(xc[c % 2, :, 0:kc], ab[pl.ds(c * kc, kc), :])
         for q in range(1, 4):
-            part += dot(xc[c % 2, q], ab[pl.ds(q * kq + c * kc, kc), :])
+            part += dot(xc[c % 2, :, q * kc:(q + 1) * kc], ab[pl.ds(q * kq + c * kc, kc), :])
         if c == 0:
             acc_s[...] = part
         else:
             acc_s[...] += part
 
     def gate_up(c, i):
-        cols = pl.ds(pl.multiple_of(i * tile, tile), tile)
-        s = dot(xc[c % 2, 0], wbuf[c % 2, 0, :, cols])
-        for q in range(1, 4):
-            s += dot(xc[c % 2, q], wbuf[c % 2, q, :, cols])
+        cols = pl.ds(i * tile, tile)
+        s = dot(xc[c % 2], wbuf[c % 2, :, cols])
         if c == 0:
             acc[:, cols] = s
         else:
@@ -219,11 +217,8 @@
         for copy in w_copies(c):
             copy.wait()
 
-        def body(i, carry):
+        for i in range(2 * f // tile):
             gate_up(c, i)
-            return carry
-
-        lax.fori_loop(0, 2 * f // tile, body, 0)
         if c + 2 < CHUNKS:
             for copy in w_copies(c + 2):
                 copy.start()
@@ -313,15 +308,12 @@
 
     load_ad.wait()
 
-    def low_block(i, carry):
-        cols = pl.ds(pl.multiple_of(i * 256, 256), 256)
-        value = dot(hbuf[0], ad[:, cols])
+    low = jnp.zeros((tokens, LANES), F32)
+    for i in range(ad.shape[1] // 256):
+        value = dot(hbuf[0], ad[:, i * 256:(i + 1) * 256])
         for h in range(2):
             owner = (2 * i + h) * slots + iota((tokens, LANES), 1) // R
-            carry += jnp.where(adapter_t == owner, value[:, h * LANES:(h + 1) * LANES], 0.0)
-        return carry
-
-    low = lax.fori_loop(0, ad.shape[1] // 256, low_block, jnp.zeros((tokens, LANES), F32))
+            low += jnp.where(adapter_t == owner, value[:, h * LANES:(h + 1) * LANES], 0.0)
     same = jnp.where(row % R == col % R, 1.0, 0.0).astype(BF16)
     low = dot(low.astype(BF16), same).astype(BF16)
     for g in range(nt):
@@ -344,31 +336,28 @@
 
     load_wd.wait()
 
-    dtile = 256 if df % 256 == 0 else LANES
-
-    def down(p, j, source, first=False):
-        lo, hi = pieces[p]
-
-        def body(i, carry):
-            cols = pl.ds(pl.multiple_of(i * dtile, dtile), dtile)
-            value = dot(hbuf[j, :, lo:hi], wd[source, lo:hi, cols])
-            if first:
-                accd[:, cols] = value
+    dtile = 512 if df % 512 == 0 else LANES
+
+    def down(p, j, source):
+        lo, hi = pieces[p] if p >= 0 else (0, f)
+        for c0 in range(0, df, dtile):
+            value = dot(hbuf[j, :, lo:hi], wd[source, lo:hi, c0:c0 + dtile])
+            if p < 0:
+                accd[:, c0:c0 + dtile] = value
             else:
-                accd[:, cols] += value
-            return carry
-
-        lax.fori_loop(0, df // dtile, body, 0)
-
+                accd[:, c0:c0 + dtile] += value
+
+    down(-1, 0, a)
     for p in range(len(pieces)):
         for j in range(1, half):
             h_copy(p, j).wait_recv()
             h_copy(p, half + j).start()
-        down(p, 0, a, p == 0)
         for j in range(1, half):
             down(p, j, (a + na - 2 * j) % na)
+        h_copy(p, half).wait_recv()
+        down(p, half, mate)
     for p in range(len(pieces)):
-        for j in range(half):
+        for j in range(1, half):
             h_copy(p, half + j).wait_recv()
             down(p, half + j, (mate + na - 2 * j) % na)
 
@@ -470,10 +459,10 @@
         out_specs=pl.BlockSpec(memory_space=pltpu.VMEM),
         scratch_shapes=[
             pltpu.VMEM((CHUNKS, n, 16, kc), BF16),
-            pltpu.VMEM((2, 4, tokens, kc), BF16),
+            pltpu.VMEM((2, tokens, 4 * kc), BF16),
             pltpu.VMEM((256, 256), BF16),
             pltpu.VMEM((2, tokens, tokens), BF16),
-            pltpu.VMEM((2, 4, kc, 2 * f), BF16),
+            pltpu.VMEM((2, 4 * kc, 2 * f), BF16),
             pltpu.VMEM((na, f, df), BF16),
             pltpu.VMEM((d_model, 2 * LANES), BF16),
             pltpu.VMEM((2, ranks // R, R, f), BF16),

time: 88 us -> 80.9 us (0.919)
  Pallas kernels: 84.8 us -> 77.7 us
    pallas_call x1, Pallas kernels: 84.8 us -> 77.7 us  [local(): pl.pallas_call(functools.partial(kernel, nt, na, pieces), out_shape=jax.S...]
where the time goes in v3:
time: 80.9 us; the launch traced here: 80.7 us
  Pallas kernels  77.7 us (96%)
  local copies, waits for them, and re-layouts  3 us (4%)
    pallas_call x1, Pallas kernels, local(): pl.pallas_call(functools.partial(kernel, nt, na, pieces), out_shape=jax.S...  77.7 us

profile of v3, /device:TPU:0, one launch (start us, length us, event | category | flops | bytes accessed | tf_op | source)
XLA Modules:
  0.0 80.7 jit_solution(8344868173006300229)
XLA Ops:
  0.0 1.5 %reshape.18.x_ref = bf16[16,2048]{1,0:T(8,128)(2,1)} reshape(bf16[4,8192]{1,0:T(4,128)(2,1)} %param.13) | data formatting | bytes 131072 | tf_op jit(solution)/shard_map/reshape | solution.py:442
  1.5 77.7 %shard_map.127 = bf16[8,16,256]{2,1,0:T(8,128)(2,1)} custom-call(bf16[16,2048]{1,0:T(8,128)(2,1)} %reshape.18.x_ref, bf16[8192,896]{1,0:T(8,128)(2,1)} %wg_ref.1, bf16[8192,896]{1,0:T(8,128)(2,1)} %wu_ref.1, bf16[8,896,1024]{2,1,0:T(8,128)(2,1)} %bitcast.6, bf16[8192,128]{1,0:T(8,128)(2,1)} %ag_ref.1, bf16[8192,128]{1,0:T(8,128)(2,1)} %au_ref.1, ...), custom_call_target="tpu_custom_call" | custom-call | tf_op jit(solution)/shard_map/pallas_call | solution.py:455
  79.2 1.5 %reshape.22 = bf16[8,4,4,256]{3,2,1,0:T(4,128)(2,1)} reshape(bf16[8,16,256]{2,1,0:T(8,128)(2,1)} %shard_map.127) | data formatting | bytes 131072 | tf_op jit(solution)/shard_map/reshape | solution.py:502

commit v4 on v3

--- a/solution.py
+++ b/solution.py
@@ -186,14 +186,11 @@
             x_start(last, c + 1)
         x_copy(last, c).wait_recv()
 
-        def arrange(g, carry):
-            block = xbuf[c, pl.ds(g * 16, 16)].reshape(256, kc)
+        for g in range(n // 16):
+            block = xbuf[c, g * 16:(g + 1) * 16].reshape(256, kc)
             value = dot(split[...], block).astype(BF16)
             for q in range(4):
-                xc[c % 2, pl.ds(pl.multiple_of(g * 64, 64), 64), q * kc:(q + 1) * kc] = value[q * 64:(q + 1) * 64]
-            return carry
-
-        lax.fori_loop(0, n // 16, arrange, 0)
+                xc[c % 2, g * 64:(g + 1) * 64, q * kc:(q + 1) * kc] = value[q * 64:(q + 1) * 64]
         if c == 0:
             load_ag.wait()
             load_au.wait()
@@ -245,26 +242,6 @@
 
     whole_chunk(CHUNKS - 2)
 
-    load_bg.wait()
-    load_bu.wait()
-    for r in range(reqs):
-        for h in range(2):
-            bsel[h, r * R:(r + 1) * R] = bgu[h, radp_ref[r]]
-    for j in range(1, na):
-        adapter_copy(shr.at[0], shr.at[j], 1, j, (a + j) % na).wait_recv()
-    shrunk = shr[0].astype(F32)
-    for j in range(1, na):
-        shrunk += shr[j].astype(F32)
-    shrunk = shrunk.astype(BF16)
-    for h in range(2):
-        parts = []
-        for g in range(4):
-            frm = (row // 32 == g) & ((row % 32) // R == h) & (row % R == col % R)
-            parts.append(dot(shrunk, jnp.where(frm, 1.0, 0.0).astype(BF16)))
-        value = jnp.concatenate(parts, axis=0)
-        value = jnp.where(request_t == iota((tokens, LANES), 1) // R, value, 0.0).astype(BF16)
-        spread[h] = dot(canon[1], value).astype(BF16)
-
     half = na // 2
     mate = flip(a, 1)
 
@@ -277,17 +254,38 @@
             send_sem=hs_sem.at[p, j], recv_sem=hr_sem.at[p, j],
             device_id=(t, target), device_id_type=MESH)
 
+    def spread_shrunk():
+        load_bg.wait()
+        load_bu.wait()
+        for r in range(reqs):
+            for h in range(2):
+                bsel[h, r * R:(r + 1) * R] = bgu[h, radp_ref[r]]
+        for j in range(1, na):
+            adapter_copy(shr.at[0], shr.at[j], 1, j, (a + j) % na).wait_recv()
+        shrunk = shr[0].astype(F32)
+        for j in range(1, na):
+            shrunk += shr[j].astype(F32)
+        shrunk = shrunk.astype(BF16)
+        for h in range(2):
+            parts = []
+            for g in range(4):
+                frm = (row // 32 == g) & ((row % 32) // R == h) & (row % R == col % R)
+                parts.append(dot(shrunk, jnp.where(frm, 1.0, 0.0).astype(BF16)))
+            value = jnp.concatenate(parts, axis=0)
+            value = jnp.where(request_t == iota((tokens, LANES), 1) // R, value, 0.0).astype(BF16)
+            spread[h] = dot(canon[1], value).astype(BF16)
+
     for copy in w_copies(CHUNKS - 1):
         copy.wait()
-    full, odd = f // 256, (f // LANES) % 2
+    made = set()
     for p, (lo, hi) in enumerate(pieces):
-        tiles = [p] if p < full else []
-        if odd and p == 0:
-            tiles.append(full)
-        if p < full:
-            tiles.append(full + odd + p)
-        for i in tiles:
+        tiles = {c0 // tile for c0 in range(lo, hi, LANES)}
+        tiles |= {(f + c0) // tile for c0 in range(lo, hi, LANES)}
+        for i in sorted(tiles - made):
             gate_up(CHUNKS - 1, i)
+        made |= tiles
+        if p == 0:
+            spread_shrunk()
         for c0 in range(lo, hi, LANES):
             gate = acc[:, c0:c0 + LANES] + dot(spread[0], bsel[0, :, c0:c0 + LANES])
             up = acc[:, f + c0:f + c0 + LANES] + dot(spread[1], bsel[1, :, c0:c0 + LANES])
@@ -297,42 +295,36 @@
         for j in range(1, half):
             h_copy(p, j).start()
 
-    for j in range(1, na):
-        br_copy(j).wait_recv()
-    rows_sum = br_recv[0].astype(F32)
-    for j in range(1, na):
-        rows_sum += br_recv[j].astype(F32)
-    br_all[t] = rows_sum.astype(BF16)
-    for j in range(1, nt):
-        tensor_copy(br_all.at[t], br_all.at[t], 0, j, (t + j) % nt).start()
-
-    load_ad.wait()
-
-    low = jnp.zeros((tokens, LANES), F32)
-    for i in range(ad.shape[1] // 256):
-        value = dot(hbuf[0], ad[:, i * 256:(i + 1) * 256])
-        for h in range(2):
-            owner = (2 * i + h) * slots + iota((tokens, LANES), 1) // R
-            low += jnp.where(adapter_t == owner, value[:, h * LANES:(h + 1) * LANES], 0.0)
-    same = jnp.where(row % R == col % R, 1.0, 0.0).astype(BF16)
-    low = dot(low.astype(BF16), same).astype(BF16)
-    for g in range(nt):
-        low_src[g] = low[g * tg:(g + 1) * tg]
-
     def low_copy(j):
         return tensor_copy(low_src.at[(t + j) % nt], low_recv.at[j], 1, j, (t + j) % nt)
 
-    for j in range(1, nt):
-        low_copy(j).start()
-    low_recv[0] = low_src[t]
-    for j in range(1, nt):
-        low_copy(j).wait_recv()
-    low_sum = low_recv[0].astype(F32)
-    for j in range(1, nt):
-        low_sum += low_recv[j].astype(F32)
-    low2[0] = low_sum.astype(BF16)
-    for j in range(1, na):
-        adapter_copy(low2.at[0], low2.at[j], 2, j, (a + j) % na).start()
+    def low_first():
+        load_ad.wait()
+
+        low = jnp.zeros((tokens, LANES), F32)
+        for i in range(ad.shape[1] // 256):
+            value = dot(hbuf[0], ad[:, i * 256:(i + 1) * 256])
+            for h in range(2):
+                owner = (2 * i + h) * slots + iota((tokens, LANES), 1) // R
+                low += jnp.where(adapter_t == owner, value[:, h * LANES:(h + 1) * LANES], 0.0)
+        same = jnp.where(row % R == col % R, 1.0, 0.0).astype(BF16)
+        low = dot(low.astype(BF16), same).astype(BF16)
+        for g in range(nt):
+            low_src[g] = low[g * tg:(g + 1) * tg]
+
+        for j in range(1, nt):
+            low_copy(j).start()
+        low_recv[0] = low_src[t]
+
+    def low_second():
+        for j in range(1, nt):
+            low_copy(j).wait_recv()
+        low_sum = low_recv[0].astype(F32)
+        for j in range(1, nt):
+            low_sum += low_recv[j].astype(F32)
+        low2[0] = low_sum.astype(BF16)
+        for j in range(1, na):
+            adapter_copy(low2.at[0], low2.at[j], 2, j, (a + j) % na).start()
 
     load_wd.wait()
 
@@ -348,14 +340,27 @@
                 accd[:, c0:c0 + dtile] += value
 
     down(-1, 0, a)
+    for j in range(1, na):
+        br_copy(j).wait_recv()
+    rows_sum = br_recv[0].astype(F32)
+    for j in range(1, na):
+        rows_sum += br_recv[j].astype(F32)
+    br_all[t] = rows_sum.astype(BF16)
+    for j in range(1, nt):
+        tensor_copy(br_all.at[t], br_all.at[t], 0, j, (t + j) % nt).start()
+
     for p in range(len(pieces)):
         for j in range(1, half):
             h_copy(p, j).wait_recv()
             h_copy(p, half + j).start()
+        if p == 0:
+            low_first()
         for j in range(1, half):
             down(p, j, (a + na - 2 * j) % na)
         h_copy(p, half).wait_recv()
         down(p, half, mate)
+        if p == 0:
+            low_second()
     for p in range(len(pieces)):
         for j in range(1, half):
             h_copy(p, half + j).wait_recv()
@@ -442,7 +447,7 @@
     x = x.reshape(tok * 4, d_model // 4)
     b_gate, b_up = b_gate.reshape(-1, R, f), b_up.reshape(-1, R, f)
     starts = [256 * p for p in range(max(f // 256, 1))]
-    pieces = tuple(zip(starts, starts[1:] + [f]))
+    pieces = tuple(zip(starts, starts[1:] + [f]))[::-1]
     n = nt * na
     kc = d_model // 4 // CHUNKS
     ranks = a_down.shape[1]

time: 80.9 us -> 83.5 us (1.032)
  Pallas kernels: 77.7 us -> 80.3 us
    pallas_call x1, Pallas kernels: 77.7 us -> 80.3 us  [local(): pl.pallas_call(functools.partial(kernel, nt, na, pieces), out_shape=jax.S...]
where the time goes in v4:
time: 83.5 us; the launch traced here: 83.3 us
  Pallas kernels  80.3 us (96%)
  local copies, waits for them, and re-layouts  3 us (4%)
    pallas_call x1, Pallas kernels, local(): pl.pallas_call(functools.partial(kernel, nt, na, pieces), out_shape=jax.S...  80.3 us

profile of v4, /device:TPU:0, one launch (start us, length us, event | category | flops | bytes accessed | tf_op | source)
XLA Modules:
  0.0 83.3 jit_solution(3102768979279264584)
XLA Ops:
  0.0 1.5 %reshape.18.x_ref = bf16[16,2048]{1,0:T(8,128)(2,1)} reshape(bf16[4,8192]{1,0:T(4,128)(2,1)} %param.13) | data formatting | bytes 131072 | tf_op jit(solution)/shard_map/reshape | solution.py:447
  1.5 80.3 %shard_map.127 = bf16[8,16,256]{2,1,0:T(8,128)(2,1)} custom-call(bf16[16,2048]{1,0:T(8,128)(2,1)} %reshape.18.x_ref, bf16[8192,896]{1,0:T(8,128)(2,1)} %wg_ref.1, bf16[8192,896]{1,0:T(8,128)(2,1)} %wu_ref.1, bf16[8,896,1024]{2,1,0:T(8,128)(2,1)} %bitcast.6, bf16[8192,128]{1,0:T(8,128)(2,1)} %ag_ref.1, bf16[8192,128]{1,0:T(8,128)(2,1)} %au_ref.1, ...), custom_call_target="tpu_custom_call" | custom-call | tf_op jit(solution)/shard_map/pallas_call | solution.py:460
  81.8 1.5 %reshape.22 = bf16[8,4,4,256]{3,2,1,0:T(4,128)(2,1)} reshape(bf16[8,16,256]{2,1,0:T(8,128)(2,1)} %shard_map.127) | data formatting | bytes 131072 | tf_op jit(solution)/shard_map/reshape | solution.py:507
